TPU v7x, 256 devices: a whole 4x4x8 slice. The times are simulated.
256 devices in a mesh: row: 8 (over z_lo, y), col: 32 (over z_hi, x, core).
Axes of the slice: x: 4, y: 4, z: 8 (z_hi: 4, z_lo: 2; z = z_hi * 2 + z_lo), core: 2. Of those that a mesh axis runs over, the one named last changes fastest.
Arguments:
- activations: bfloat16 [1024, 8192], P('col', 'row'), may hold values from -6 to 6
- cotangent: bfloat16 [1024, 8192], P('col', 'row'), may hold values from -0.59765625 to 0.59765625
- gate_weight: bfloat16 [8192, 21504], P('row', 'col'), may hold values from -0.0625 to 0.0625
- up_weight: bfloat16 [8192, 21504], P('row', 'col'), may hold values from -0.0625 to 0.0625
- down_weight: bfloat16 [21504, 8192], P('col', 'row'), may hold values from -0.0390625 to 0.0390625
Outputs:
- input_grad: bfloat16 [1024, 8192], P('col', 'row')
- gate_grad: bfloat16 [8192, 21504], P('row', 'col')
- up_grad: bfloat16 [8192, 21504], P('row', 'col')
- down_grad: bfloat16 [21504, 8192], P('col', 'row')
All inputs are finite; a program needn't handle non-finite values.
Results may differ from a plain program's by a relative error of at most 0.005.
Values may be sent and summed in bfloat16 or wider, within the bound.
No kernel may reach another device: no remote copies, remote signals or barrier semaphores. Data moves between devices by JAX's collectives and lax.ppermute only.
A program may use at most 128 MiB of HBM per device.

v0:
```python
import jax
import jax.numpy as jnp
from jax import lax
from jax.sharding import PartitionSpec as P


def local_deltas(sums, hid_cols):
    gate = sums[:, :hid_cols]
    up = sums[:, hid_cols : 2 * hid_cols]
    hidden_grad = sums[:, 2 * hid_cols :]
    sigmoid_gate = jax.nn.sigmoid(gate)
    hidden = (gate * sigmoid_gate * up).astype(jnp.bfloat16)
    gate_delta = (hidden_grad * up * sigmoid_gate * (1.0 + gate * (1.0 - sigmoid_gate))).astype(
        jnp.bfloat16
    )
    up_delta = (hidden_grad * gate * sigmoid_gate).astype(jnp.bfloat16)
    return (hidden, gate_delta, up_delta)


def per_device(activations, cotangent, gate_weight, up_weight, down_weight):
    act_all, cot_all = (
        lax.all_gather(activations, "col", axis=0, tiled=True),
        lax.all_gather(cotangent, "col", axis=0, tiled=True),
    )
    hid_cols = gate_weight.shape[1]
    both_weights = jnp.concatenate([gate_weight, up_weight], axis=1)
    contract_cols = (((1,), (1,)), ((), ()))
    contract_rows = (((0,), (0,)), ((), ()))
    forward_part = jnp.dot(act_all, both_weights, preferred_element_type=jnp.float32)
    backward_part = lax.dot_general(
        cot_all, down_weight, contract_cols, preferred_element_type=jnp.float32
    )
    sums = lax.psum_scatter(
        jnp.concatenate([forward_part, backward_part], axis=1),
        "row",
        scatter_dimension=0,
        tiled=True,
    )
    hidden, gate_delta, up_delta = local_deltas(sums, hid_cols)
    hidden, gate_delta, up_delta = (
        lax.all_gather(hidden, "row", axis=0, tiled=True),
        lax.all_gather(gate_delta, "row", axis=0, tiled=True),
        lax.all_gather(up_delta, "row", axis=0, tiled=True),
    )
    down_grad = lax.dot_general(
        hidden, cot_all, contract_rows, preferred_element_type=jnp.float32
    ).astype(jnp.bfloat16)
    gate_grad = lax.dot_general(
        act_all, gate_delta, contract_rows, preferred_element_type=jnp.float32
    ).astype(jnp.bfloat16)
    up_grad = lax.dot_general(
        act_all, up_delta, contract_rows, preferred_element_type=jnp.float32
    ).astype(jnp.bfloat16)
    both_deltas = jnp.concatenate([gate_delta, up_delta], axis=1)
    input_grad = lax.psum_scatter(
        lax.dot_general(
            both_deltas, both_weights, contract_cols, preferred_element_type=jnp.float32
        ),
        "col",
        scatter_dimension=0,
        tiled=True,
    )
    return (input_grad.astype(jnp.bfloat16), gate_grad, up_grad, down_grad)


def solution(mesh):
    return jax.shard_map(
        per_device,
        mesh=mesh,
        in_specs=(
            P("col", "row"),
            P("col", "row"),
            P("row", "col"),
            P("row", "col"),
            P("col", "row"),
        ),
        out_specs=(P("col", "row"), P("row", "col"), P("row", "col"), P("col", "row")),
        check_vma=False,
    )
```

profile of v0, /device:TPU:8, one launch (start us, length us, event | category | flops | bytes accessed | tf_op | source)
XLA Modules:
  0.0 472.7 jit_solution(8116359554584954687)
XLA Ops:
  7.2 0.0 all-gather.8.cloned.1.call-start
  7.2 0.7 all-gather.8.cloned.1.call-update
  7.9 0.0 all-gather.6.cloned.1.call-start
  8.0 0.7 all-gather.6.cloned.1.call-update
  8.7 0.0 reduce-scatter.3.cloned.1.call-start
  8.7 2.6 constant_dynamic-update-slice_fusion.1
  11.3 1.2 constant_dynamic-update-slice_fusion
  12.5 55.7 %all-gather.8.cloned.1.call-done = bf16[1024,1024]{1,0:T(8,128)(2,1)} async-done(((bf16[32,1024]{1,0:T(8,128)(2,1)}), bf16[1024,1024]{1,0:T(8,128)(2,1)}) %all-gather.8.cloned.1.call-update) | async-done | bytes 2097168 | tf_op jit(solution)/shard_map/all_gather | solution.py:23
  68.2 4.8 %fusion.7 = f32[1024,672]{0,1:T(8,128)} fusion(bf16[1024,1024]{1,0:T(8,128)(2,1)} %all-gather.8.cloned.1.call-done, bf16[672,1024]{1,0:T(8,128)(2,1)S(1)} %copy-done), kind=kOutput, calls=%fused_computation.18 | convolution fusion | flops 1409286144 | bytes 6225920 | tf_op jit(solution)/shard_map/dot_general | solution.py:30
  73.0 49.5 %all-gather.6.cloned.1.call-done = bf16[1024,1024]{1,0:T(8,128)(2,1)} async-done(((bf16[32,1024]{1,0:T(8,128)(2,1)}), bf16[1024,1024]{1,0:T(8,128)(2,1)}) %all-gather.6.cloned.1.call-update) | async-done | bytes 2097168 | tf_op jit(solution)/shard_map/all_gather | solution.py:22
  122.4 5.6 %convolution_bitcast_fusion = f32[1024,1344]{0,1:T(8,128)S(1)} fusion(bf16[1024,1344]{0,1:T(8,128)(2,1)} %constant_dynamic-update-slice_fusion, bf16[1024,1024]{1,0:T(8,128)(2,1)} %all-gather.6.cloned.1.call-done), kind=kOutput, calls=%fused_computation.1 | convolution fusion | flops 2818572288 | bytes 10354688 | tf_op jit(solution)/shard_map/dot_general | solution.py:29
  128.1 4.9 %pad_maximum_fusion = f32[1024,2016]{0,1:T(8,128)} fusion(f32[1024,672]{0,1:T(8,128)S(1)} %copy-done.1, f32[1024,1344]{0,1:T(8,128)S(1)} %convolution_bitcast_fusion), kind=kLoop, calls=%fused_computation | loop fusion | flops 2064384 | bytes 16515072 | tf_op jit(solution)/shard_map/concatenate | solution.py:34
  133.0 0.0 reduce-scatter.3.cloned.1.call-update
  133.0 0.0 all-gather.10.cloned.1.call-start
  133.1 89.0 %reduce-scatter.3.cloned.1.call-done = f32[128,2016]{0,1:T(8,128)} async-done(((f32[1024,2016]{0,1:T(8,128)}), f32[128,2016]{0,1:T(8,128)}) %reduce-scatter.3.cloned.1.call-update) | async-done | bytes 1032208 | tf_op jit(solution)/shard_map/reduce_scatter | solution.py:33
  222.0 2.1 multiply_convert_fusion
  224.1 0.0 all-gather.10.cloned.1.call-update
  224.2 0.0 all-gather.12.cloned.1.call-start
  224.2 0.5 all-gather.12.cloned.1.call-update
  224.8 0.0 all-gather.14.cloned.1.call-start
  224.8 0.5 all-gather.14.cloned.1.call-update
  225.3 0.2 reduce-scatter.5.cloned.1.call-start
  225.6 41.6 %all-gather.10.cloned.1.call-done = bf16[1024,672]{0,1:T(8,128)(2,1)} async-done(((bf16[128,672]{0,1:T(8,128)(2,1)}), bf16[1024,672]{0,1:T(8,128)(2,1)}) %all-gather.10.cloned.1.call-update) | async-done | bytes 1376272 | tf_op jit(solution)/shard_map/all_gather | solution.py:42
  267.2 45.7 %all-gather.12.cloned.1.call-done = bf16[1024,672]{0,1:T(8,128)(2,1)} async-done(((bf16[128,672]{0,1:T(8,128)(2,1)}), bf16[1024,672]{0,1:T(8,128)(2,1)}) %all-gather.12.cloned.1.call-update) | async-done | bytes 1376272 | tf_op jit(solution)/shard_map/all_gather | solution.py:43
  312.9 8.2 %fusion = f32[1024,1024]{1,0:T(8,128)} fusion(bf16[1024,1344]{0,1:T(8,128)(2,1)} %constant_dynamic-update-slice_fusion, bf16[1024,672]{0,1:T(8,128)(2,1)} %all-gather.12.cloned.1.call-done, bf16[1024,672]{0,1:T(8,128)(2,1)} %all-gather.10.cloned.1.call-done), kind=kOutput, calls=%fused_computation.2 | convolution fusion | flops 2824077312 | bytes 9699328 | tf_op jit(solution)/shard_map/dot_general | solution.py:56
  321.1 1.6 copy-done.4
  322.6 4.2 fusion.5
  326.8 2.7 fusion.4
  329.5 29.1 %all-gather.14.cloned.1.call-done = bf16[1024,672]{0,1:T(8,128)(2,1)} async-done(((bf16[128,672]{0,1:T(8,128)(2,1)}), bf16[1024,672]{0,1:T(8,128)(2,1)}) %all-gather.14.cloned.1.call-update) | async-done | bytes 1376272 | tf_op jit(solution)/shard_map/all_gather | solution.py:41
  358.6 4.0 convolution_convert_fusion
  362.6 101.8 %reduce-scatter.5.cloned.1.call-done = f32[32,1024]{1,0:T(8,128)} async-done(((f32[1024,1024]{1,0:T(8,128)}), f32[32,1024]{1,0:T(8,128)}) %reduce-scatter.5.cloned.1.call-update) | async-done | bytes 131088 | tf_op jit(solution)/shard_map/reduce_scatter | solution.py:55
  464.4 1.5 convert_element_type.29
  (14 shorter events, 0.0 us)
Async XLA Ops:
  7.2 61.0 %copy-start = (bf16[672,1024]{1,0:T(8,128)(2,1)S(1)}, bf16[672,1024]{1,0:T(8,128)(2,1)}, u32[]{:S(2)}) copy-start(bf16[672,1024]{1,0:T(8,128)(2,1)} %param.9) | copy-start | bytes 4128772
  7.2 4.1 copy-start.2
  7.2 61.0 %all-gather.8.cloned.1.call-start = ((), (), s32[]{:S(2)}) async-start(), calls=%async_computation.3 | async-start | bytes 2162688 | tf_op jit(solution)/shard_map/all_gather | solution.py:23
  7.9 114.5 %all-gather.6.cloned.1.call-start = ((), (), s32[]{:S(2)}) async-start(), calls=%async_computation.2 | async-start | bytes 2162688 | tf_op jit(solution)/shard_map/all_gather | solution.py:22
  8.7 213.3 %reduce-scatter.3.cloned.1.call-start = ((), (), s32[]{:S(2)}) async-start(), calls=%async_computation.4 | async-start | bytes 9289728 | tf_op jit(solution)/shard_map/reduce_scatter | solution.py:33
  122.4 5.6 %copy-start.1 = (f32[1024,672]{0,1:T(8,128)S(1)}, f32[1024,672]{0,1:T(8,128)}, u32[]{:S(2)}) copy-start(f32[1024,672]{0,1:T(8,128)} %fusion.7) | copy-start | bytes 8257540
  133.0 134.2 %all-gather.10.cloned.1.call-start = ((), (), s32[]{:S(2)}) async-start(), calls=%async_computation.5 | async-start | bytes 1548288 | tf_op jit(solution)/shard_map/all_gather | solution.py:42
  224.2 88.7 %all-gather.12.cloned.1.call-start = ((), (), s32[]{:S(2)}) async-start(), calls=%async_computation.6 | async-start | bytes 1548288 | tf_op jit(solution)/shard_map/all_gather | solution.py:43
  224.8 133.8 %all-gather.14.cloned.1.call-start = ((), (), s32[]{:S(2)}) async-start(), calls=%async_computation.8 | async-start | bytes 1548288 | tf_op jit(solution)/shard_map/all_gather | solution.py:41
  225.3 239.0 %reduce-scatter.5.cloned.1.call-start = ((), (), s32[]{:S(2)}) async-start(), calls=%async_computation.7 | async-start | bytes 4325376 | tf_op jit(solution)/shard_map/reduce_scatter | solution.py:55
  321.0 1.6 copy-start.4
  322.6 4.2 copy-start.5
  322.6 4.2 copy-start.6
  326.8 31.8 %copy-start.3 = (bf16[1024,1024]{1,0:T(8,128)(2,1)S(1)}, bf16[1024,1024]{1,0:T(8,128)(2,1)}, u32[]{:S(2)}) copy-start(bf16[1024,1024]{1,0:T(8,128)(2,1)} %all-gather.8.cloned.1.call-done) | copy-start | bytes 6291460
Sparse Core Ops, SparseCore 0:
  10.6 57.5 all-gather.7
  70.7 51.6 all-gather.5
  133.1 88.8 reduce-scatter.2
  224.3 42.8 all-gather.9
  269.4 43.3 all-gather.11
  315.1 43.3 all-gather.13
  363.0 101.3 reduce-scatter.4
where the time goes:
time: 473 us
  waiting for transfers between devices  415 us (88%)
  matrix products  29.4 us (6%)
  between operations  14.2 us (3%)
  other arithmetic  8.58 us (2%)
  local copies, waits for them, and re-layouts  5.38 us (1%)
    reduce_scatter x1, waiting for transfers between devices, per_device(): lax.psum_scatter(lax.dot_general(both_deltas, both_weights, contract_cols...  102 us
    reduce_scatter x1, waiting for transfers between devices, per_device(): lax.psum_scatter(jnp.concatenate([forward_part, backward_part], axis=1),...  89 us
    all_gather x1, waiting for transfers between devices, per_device(): lax.all_gather(cotangent, 'col', axis=0, tiled=True)  55.7 us
    all_gather x1, waiting for transfers between devices, per_device(): lax.all_gather(activations, 'col', axis=0, tiled=True)  49.5 us
    all_gather x1, waiting for transfers between devices, per_device(): lax.all_gather(up_delta, 'row', axis=0, tiled=True)  45.7 us
    all_gather x1, waiting for transfers between devices, per_device(): lax.all_gather(gate_delta, 'row', axis=0, tiled=True)  41.6 us
    all_gather x1, waiting for transfers between devices, per_device(): lax.all_gather(hidden, 'row', axis=0, tiled=True)  29.1 us
  transfers between devices with their start and end apart: 7, of which 7 were waited for; matrix products, arithmetic and copies ran while one was open for 6% of the time, Pallas kernels for 0%

commit v1 on v0

--- a/solution.py
+++ b/solution.py
@@ -2,6 +2,11 @@
 import jax.numpy as jnp
 from jax import lax
 from jax.sharding import PartitionSpec as P
+
+
+def gather_over(block, axis, d):
+    sent = jnp.stack([block] * lax.axis_size(axis))
+    return jnp.concatenate(lax.all_to_all(sent, axis, 0, 0), axis=d)
 
 
 def local_deltas(sums, hid_cols):
@@ -20,7 +25,7 @@
 def per_device(activations, cotangent, gate_weight, up_weight, down_weight):
     act_all, cot_all = (
         lax.all_gather(activations, "col", axis=0, tiled=True),
-        lax.all_gather(cotangent, "col", axis=0, tiled=True),
+        gather_over(cotangent, "col", 0),
     )
     hid_cols = gate_weight.shape[1]
     both_weights = jnp.concatenate([gate_weight, up_weight], axis=1)

time: 473 us -> 439 us (0.928)
  waiting for transfers between devices: 415 us -> 370 us
  starting transfers between devices: 0.45 us -> 11.7 us
    all_gather x1 -> x0, waiting for transfers between devices: 55.7 us -> none  [per_device(): lax.all_gather(cotangent, 'col', axis=0, tiled=True)]
    all_to_all x0 -> x1, waiting for transfers between devices: none -> 49 us  [gather_over(): return jnp.concatenate(lax.all_to_all(sent, axis, 0, 0), axis=d)]
    all_gather x1, waiting for transfers between devices: 49.5 us -> 10.4 us  [per_device(): lax.all_gather(activations, 'col', axis=0, tiled=True)]
    all_to_all x0 -> x1, starting transfers between devices: none -> 11.3 us  [gather_over(): return jnp.concatenate(lax.all_to_all(sent, axis, 0, 0), axis=d)]
where the time goes in v1:
time: 439 us
  waiting for transfers between devices  370 us (84%)
  matrix products  28.4 us (6%)
  between operations  14.2 us (3%)
  starting transfers between devices  11.7 us (3%)
  other arithmetic  8.56 us (2%)
  local copies, waits for them, and re-layouts  6.43 us (1%)
    reduce_scatter x1, waiting for transfers between devices, per_device(): lax.psum_scatter(lax.dot_general(both_deltas, both_weights, contract_cols...  102 us
    reduce_scatter x1, waiting for transfers between devices, per_device(): lax.psum_scatter(jnp.concatenate([forward_part, backward_part], axis=1),...  89.4 us
    all_to_all x1, waiting for transfers between devices, gather_over(): return jnp.concatenate(lax.all_to_all(sent, axis, 0, 0), axis=d)  49 us
    all_gather x1, waiting for transfers between devices, per_device(): lax.all_gather(up_delta, 'row', axis=0, tiled=True)  45.7 us
    all_gather x1, waiting for transfers between devices, per_device(): lax.all_gather(gate_delta, 'row', axis=0, tiled=True)  41.8 us
    all_gather x1, waiting for transfers between devices, per_device(): lax.all_gather(hidden, 'row', axis=0, tiled=True)  30 us
    all_to_all x1, starting transfers between devices, gather_over(): return jnp.concatenate(lax.all_to_all(sent, axis, 0, 0), axis=d)  11.3 us
    all_gather x1, waiting for transfers between devices, per_device(): lax.all_gather(activations, 'col', axis=0, tiled=True)  10.4 us
  transfers between devices with their start and end apart: 7, of which 7 were waited for; matrix products, arithmetic and copies ran while one was open for 6% of the time, Pallas kernels for 0%

profile of v1, /device:TPU:8, one launch (start us, length us, event | category | flops | bytes accessed | tf_op | source)
XLA Modules:
  0.0 439.0 jit_solution(16829743270430711331)
XLA Ops:
  7.2 2.6 stack.2
  9.7 11.3 %all-to-all-start = ((bf16[32,32,1024]{2,1,0:T(8,128)(2,1)}), bf16[32,32,1024]{2,1,0:T(8,128)(2,1)S(1)}, u32[]{:S(2)}, u32[]{:S(2)}) async-start(bf16[32,32,1024]{2,1,0:T(8,128)(2,1)} %stack.2), calls=%async_computation | async-start | bytes 4194304 | tf_op jit(solution)/shard_map/all_to_all | solution.py:9
  21.1 0.0 all-gather.5.cloned.1.call-start
  21.1 0.7 all-gather.5.cloned.1.call-update
  21.8 0.0 reduce-scatter.3.cloned.1.call-start
  21.9 2.6 constant_dynamic-update-slice_fusion.1
  24.5 1.2 constant_dynamic-update-slice_fusion
  25.7 49.0 %all-to-all-done = bf16[32,32,1024]{2,1,0:T(8,128)(2,1)S(1)} async-done(((bf16[32,32,1024]{2,1,0:T(8,128)(2,1)}), bf16[32,32,1024]{2,1,0:T(8,128)(2,1)S(1)}, u32[]{:S(2)}, u32[]{:S(2)}) %all-to-all-start) | async-done | bytes 2097184 | tf_op jit(solution)/shard_map/all_to_all | solution.py:9
  74.7 3.2 fusion.7
  77.8 10.4 %all-gather.5.cloned.1.call-done = bf16[1024,1024]{1,0:T(8,128)(2,1)} async-done(((bf16[32,1024]{1,0:T(8,128)(2,1)}), bf16[1024,1024]{1,0:T(8,128)(2,1)}) %all-gather.5.cloned.1.call-update) | async-done | bytes 2097168 | tf_op jit(solution)/shard_map/all_gather | solution.py:27
  88.2 5.6 %convolution_bitcast_fusion = f32[1024,1344]{0,1:T(8,128)S(1)} fusion(bf16[1024,1344]{0,1:T(8,128)(2,1)} %constant_dynamic-update-slice_fusion, bf16[1024,1024]{1,0:T(8,128)(2,1)} %all-gather.5.cloned.1.call-done), kind=kOutput, calls=%fused_computation.1 | convolution fusion | flops 2818572288 | bytes 10354688 | tf_op jit(solution)/shard_map/dot_general | solution.py:34
  93.9 4.9 %pad_maximum_fusion = f32[1024,2016]{0,1:T(8,128)} fusion(f32[1024,672]{0,1:T(8,128)S(1)} %copy-done.1, f32[1024,1344]{0,1:T(8,128)S(1)} %convolution_bitcast_fusion), kind=kLoop, calls=%fused_computation | loop fusion | flops 2064384 | bytes 16515072 | tf_op jit(solution)/shard_map/concatenate | solution.py:39
  98.8 0.0 reduce-scatter.3.cloned.1.call-update
  98.8 0.0 all-gather.7.cloned.1.call-start
  98.8 89.4 %reduce-scatter.3.cloned.1.call-done = f32[128,2016]{0,1:T(8,128)} async-done(((f32[1024,2016]{0,1:T(8,128)}), f32[128,2016]{0,1:T(8,128)}) %reduce-scatter.3.cloned.1.call-update) | async-done | bytes 1032208 | tf_op jit(solution)/shard_map/reduce_scatter | solution.py:38
  188.2 2.1 multiply_convert_fusion
  190.4 0.0 all-gather.7.cloned.1.call-update
  190.4 0.0 all-gather.9.cloned.1.call-start
  190.4 0.5 all-gather.9.cloned.1.call-update
  191.0 0.0 all-gather.11.cloned.1.call-start
  191.0 0.5 all-gather.11.cloned.1.call-update
  191.5 0.2 reduce-scatter.5.cloned.1.call-start
  191.8 41.8 %all-gather.7.cloned.1.call-done = bf16[1024,672]{0,1:T(8,128)(2,1)} async-done(((bf16[128,672]{0,1:T(8,128)(2,1)}), bf16[1024,672]{0,1:T(8,128)(2,1)}) %all-gather.7.cloned.1.call-update) | async-done | bytes 1376272 | tf_op jit(solution)/shard_map/all_gather | solution.py:47
  233.5 45.7 %all-gather.9.cloned.1.call-done = bf16[1024,672]{0,1:T(8,128)(2,1)} async-done(((bf16[128,672]{0,1:T(8,128)(2,1)}), bf16[1024,672]{0,1:T(8,128)(2,1)}) %all-gather.9.cloned.1.call-update) | async-done | bytes 1376272 | tf_op jit(solution)/shard_map/all_gather | solution.py:48
  279.2 8.1 %fusion = f32[1024,1024]{1,0:T(8,128)} fusion(bf16[1024,1344]{0,1:T(8,128)(2,1)} %constant_dynamic-update-slice_fusion, bf16[1024,672]{0,1:T(8,128)(2,1)} %all-gather.9.cloned.1.call-done, bf16[1024,672]{0,1:T(8,128)(2,1)} %all-gather.7.cloned.1.call-done), kind=kOutput, calls=%fused_computation.2 | convolution fusion | flops 2824077312 | bytes 9699328 | tf_op jit(solution)/shard_map/dot_general | solution.py:61
  287.4 0.0 reduce-scatter.5.cloned.1.call-update
  287.4 4.8 %fusion.5 = bf16[1024,672]{0,1:T(8,128)(2,1)} fusion(bf16[1024,672]{0,1:T(8,128)(2,1)} %all-gather.9.cloned.1.call-done, bf16[1024,1024]{1,0:T(8,128)(2,1)} %all-gather.5.cloned.1.call-done), kind=kOutput, calls=%fused_computation.10 | convolution fusion | flops 1409974272 | bytes 4849664 | tf_op jit(solution)/shard_map/dot_general | solution.py:56
  292.2 2.7 fusion.4
  294.9 30.0 %all-gather.11.cloned.1.call-done = bf16[1024,672]{0,1:T(8,128)(2,1)} async-done(((bf16[128,672]{0,1:T(8,128)(2,1)}), bf16[1024,672]{0,1:T(8,128)(2,1)}) %all-gather.11.cloned.1.call-update) | async-done | bytes 1376272 | tf_op jit(solution)/shard_map/all_gather | solution.py:46
  324.9 4.0 convolution_convert_fusion
  328.9 101.6 %reduce-scatter.5.cloned.1.call-done = f32[32,1024]{1,0:T(8,128)} async-done(((f32[1024,1024]{1,0:T(8,128)}), f32[32,1024]{1,0:T(8,128)}) %reduce-scatter.5.cloned.1.call-update) | async-done | bytes 131088 | tf_op jit(solution)/shard_map/reduce_scatter | solution.py:60
  430.6 1.5 convert_element_type.29
  (10 shorter events, 0.0 us)
Async XLA Ops:
  7.2 67.5 %copy-start = (bf16[672,1024]{1,0:T(8,128)(2,1)S(1)}, bf16[672,1024]{1,0:T(8,128)(2,1)}, u32[]{:S(2)}) copy-start(bf16[672,1024]{1,0:T(8,128)(2,1)} %param.9) | copy-start | bytes 4128772
  9.7 64.9 %all-to-all-start = ((bf16[32,32,1024]{2,1,0:T(8,128)(2,1)}), bf16[32,32,1024]{2,1,0:T(8,128)(2,1)S(1)}, u32[]{:S(2)}, u32[]{:S(2)}) async-start(bf16[32,32,1024]{2,1,0:T(8,128)(2,1)} %stack.2), calls=%async_computation | async-start | bytes 4194304 | tf_op jit(solution)/shard_map/all_to_all | solution.py:9
  21.1 67.2 %all-gather.5.cloned.1.call-start = ((), (), s32[]{:S(2)}) async-start(), calls=%async_computation.3 | async-start | bytes 2162688 | tf_op jit(solution)/shard_map/all_gather | solution.py:27
  21.8 166.4 %reduce-scatter.3.cloned.1.call-start = ((), (), s32[]{:S(2)}) async-start(), calls=%async_computation.4 | async-start | bytes 9289728 | tf_op jit(solution)/shard_map/reduce_scatter | solution.py:38
  21.9 2.6 copy-start.2
  88.2 5.6 %copy-start.1 = (f32[1024,672]{0,1:T(8,128)S(1)}, f32[1024,672]{0,1:T(8,128)}, u32[]{:S(2)}) copy-start(f32[1024,672]{0,1:T(8,128)} %fusion.7) | copy-start | bytes 8257540
  98.8 134.8 %all-gather.7.cloned.1.call-start = ((), (), s32[]{:S(2)}) async-start(), calls=%async_computation.5 | async-start | bytes 1548288 | tf_op jit(solution)/shard_map/all_gather | solution.py:47
  190.4 88.9 %all-gather.9.cloned.1.call-start = ((), (), s32[]{:S(2)}) async-start(), calls=%async_computation.6 | async-start | bytes 1548288 | tf_op jit(solution)/shard_map/all_gather | solution.py:48
  191.0 134.0 %all-gather.11.cloned.1.call-start = ((), (), s32[]{:S(2)}) async-start(), calls=%async_computation.8 | async-start | bytes 1548288 | tf_op jit(solution)/shard_map/all_gather | solution.py:46
  191.5 239.0 %reduce-scatter.5.cloned.1.call-start = ((), (), s32[]{:S(2)}) async-start(), calls=%async_computation.7 | async-start | bytes 4325376 | tf_op jit(solution)/shard_map/reduce_scatter | solution.py:60
  287.4 4.8 %copy-start.3 = (bf16[1024,1024]{1,0:T(8,128)(2,1)S(1)}, bf16[1024,1024]{1,0:T(8,128)(2,1)}, u32[]{:S(2)}) copy-start(bf16[1024,1024]{1,0:T(8,128)(2,1)} %all-gather.5.cloned.1.call-done) | copy-start | bytes 6291460
  287.4 4.8 %copy-start.4 = (bf16[1024,672]{0,1:T(8,128)(2,1)S(1)}, bf16[1024,672]{0,1:T(8,128)(2,1)}, u32[]{:S(2)}) copy-start(bf16[1024,672]{0,1:T(8,128)(2,1)} %all-gather.7.cloned.1.call-done) | copy-start | bytes 4128772
Sparse Core Ops, SparseCore 0:
  24.5 63.7 all-gather.4
  98.9 89.2 reduce-scatter.2
  190.6 42.8 all-gather.6
  235.8 43.3 all-gather.8
  281.5 43.3 all-gather.10
  329.2 101.3 reduce-scatter.4
